TPU v7x, 256 devices: a whole 4x4x8 slice. The times are simulated.
256 devices in a mesh: stn: 32 (over z, x), tm: 8 (over y, core).
Axes of the slice: x: 4, y: 4, z: 8, core: 2. Of those that a mesh axis runs over, the one named last changes fastest.
Arguments:
- streams: bfloat16 [2, 32, 4194304], P(None, 'stn', 'tm'), may hold values from -6 to 6
- sample_delays: int32 [32], P('stn'), may hold values from 0 to 2048, as said below
- fringe_rates: int32 [32], P('stn'), may hold values from -32768 to 32768
Outputs:
- visibilities: float32 [2, 32, 32, 4096], P(None, 'tm', None, 'stn')
- auto_spectra: float32 [32, 4096], P('tm', 'stn')
Inputs may be any that keep to these rules, and one draw needn't show every extreme that they name: `sample_delays`: one station's delay is exactly 2048.
All inputs are finite; a program needn't handle non-finite values.
Results may differ from a plain program's by a relative error of at most 0.0082.
Values may be sent and summed in bfloat16 or wider, within the bound.
A program may use at most 64 MiB of HBM per device.

v0:
```python
import math

import jax
import jax.numpy as jnp
from jax import lax
from jax.sharding import PartitionSpec as P

FAC_A = 16
FAC_B = 256
NCH = 4096
MAXD = 2048
FRAMES_DEV = 128


two_pi = 2.0 * math.pi
turn_split = 1024
full_turn = 1048576.0


def from_behind(array, axis, by):
    length = lax.axis_size(axis)
    pairs = [(i, i + by) for i in range(length) if 0 <= i + by < length]
    return lax.ppermute(array, axis, pairs)


def phase_turns(rate_col, times):
    upper = times // turn_split
    lower = times % turn_split
    high = jnp.mod(rate_col * upper, turn_split)
    return jnp.mod(high * turn_split + rate_col * lower, turn_split * turn_split)


def dft_tables():
    first_idx = jnp.arange(FAC_A, dtype=jnp.int32)
    second_idx = jnp.arange(FAC_B, dtype=jnp.int32)
    angle_first = two_pi * (
        jnp.mod(first_idx[:, None] * first_idx[None, :], FAC_A).astype(jnp.float32) / FAC_A
    )
    angle_twiddle = two_pi * (
        jnp.mod(first_idx[:, None] * second_idx[None, :], NCH).astype(jnp.float32) / NCH
    )
    angle_second = two_pi * (
        jnp.mod(second_idx[:, None] * second_idx[None, :], FAC_B).astype(jnp.float32) / FAC_B
    )
    norm_scale = 1.0 / math.sqrt(NCH)
    return (
        jnp.cos(angle_first).astype(jnp.bfloat16),
        jnp.sin(angle_first).astype(jnp.bfloat16),
        jnp.cos(angle_twiddle) * norm_scale,
        jnp.sin(angle_twiddle) * norm_scale,
        jnp.cos(angle_second).astype(jnp.bfloat16),
        jnp.sin(angle_second).astype(jnp.bfloat16),
    )


def rotate(real_in, imag_in, rate_vec, times):
    turns = phase_turns(rate_vec[:, None], times[None, :])
    angle = two_pi * turns.astype(jnp.float32) / full_turn
    cosine = jnp.cos(angle)
    sine = jnp.sin(angle)
    real_out = (real_in * cosine + imag_in * sine).astype(jnp.bfloat16)
    imag_out = (imag_in * cosine - real_in * sine).astype(jnp.bfloat16)
    return (real_out, imag_out)


def first_section(data, table):
    return jnp.einsum("sfan,ak->sfkn", data, table, preferred_element_type=jnp.float32)


def second_section(data, table):
    return jnp.einsum("sfkn,nm->sfmk", data, table, preferred_element_type=jnp.float32)


def channelize(real_in, imag_in, tables):
    cos_first, sin_first, cos_twid, sin_twid, cos_second, sin_second = tables
    stations, length = real_in.shape
    frames = length // NCH
    real_frames = real_in.reshape(stations, frames, FAC_A, FAC_B)
    imag_frames = imag_in.reshape(stations, frames, FAC_A, FAC_B)
    part_real = first_section(real_frames, cos_first) + first_section(imag_frames, sin_first)
    part_imag = first_section(imag_frames, cos_first) - first_section(real_frames, sin_first)
    turn_real = (part_real * cos_twid + part_imag * sin_twid).astype(jnp.bfloat16)
    turn_imag = (part_imag * cos_twid - part_real * sin_twid).astype(jnp.bfloat16)
    spec_real = second_section(turn_real, cos_second) + second_section(turn_imag, sin_second)
    spec_imag = second_section(turn_imag, cos_second) - second_section(turn_real, sin_second)
    return jnp.stack(
        [
            spec_real.reshape(stations, frames, NCH).astype(jnp.bfloat16),
            spec_imag.reshape(stations, frames, NCH).astype(jnp.bfloat16),
        ]
    )


def correlate(spectra):
    left_real = spectra[0]
    left_imag = spectra[1]
    corr_real = jnp.einsum(
        "sfc,tfc->stc", left_real, left_real, preferred_element_type=jnp.float32
    ) + jnp.einsum("sfc,tfc->stc", left_imag, left_imag, preferred_element_type=jnp.float32)
    corr_imag = jnp.einsum(
        "sfc,tfc->stc", left_imag, left_real, preferred_element_type=jnp.float32
    ) - jnp.einsum("sfc,tfc->stc", left_real, left_imag, preferred_element_type=jnp.float32)
    return jnp.stack([corr_real, corr_imag])


def per_device(streams, sample_delays, fringe_rates):
    slice_len = streams.shape[2]
    rim_samples = from_behind(streams[:, :, :MAXD], "tm", -1)
    extended = jnp.concatenate([streams, rim_samples], axis=2)
    pieces = jax.vmap(
        lambda stream_row, shift_by: lax.dynamic_slice_in_dim(stream_row, shift_by, slice_len, 1),
        in_axes=(1, 0),
        out_axes=1,
    )(extended, sample_delays)
    time_index = lax.axis_index("tm")
    times = time_index * slice_len + jnp.arange(slice_len, dtype=jnp.int32)
    real_rot, imag_rot = rotate(
        pieces[0].astype(jnp.float32), pieces[1].astype(jnp.float32), fringe_rates, times
    )
    spectra = channelize(real_rot, imag_rot, dft_tables())
    owned = lax.all_to_all(spectra, "stn", split_axis=3, concat_axis=1, tiled=True)
    summed = lax.psum_scatter(correlate(owned), "tm", scatter_dimension=1, tiled=True)
    row_count = summed.shape[1]
    station_count = summed.shape[2]
    frame_total = FRAMES_DEV * lax.axis_size("tm")
    row_global = time_index * row_count + jnp.arange(row_count, dtype=jnp.int32)
    identity = (row_global[:, None] == jnp.arange(station_count, dtype=jnp.int32)[None, :]).astype(
        jnp.float32
    )
    off_diag = (1.0 - identity)[None, :, :, None]
    visibilities = summed * off_diag * (1.0 / math.sqrt(frame_total))
    auto_spectra = jnp.sum(summed[0] * identity[:, :, None], axis=1) / frame_total
    return (visibilities, auto_spectra)


def solution(mesh):
    in_specs = (P(None, "stn", "tm"), P("stn"), P("stn"))
    out_specs = (P(None, "tm", None, "stn"), P("tm", "stn"))
    return jax.shard_map(
        per_device, mesh=mesh, in_specs=in_specs, out_specs=out_specs, check_vma=False
    )
```

profile of v0, /device:TPU:1, one launch (start us, length us, event | category | flops | bytes accessed | tf_op | source)
XLA Modules:
  0.0 209.4 jit_solution(6625159570368863065)
XLA Ops:
  7.2 0.0 reduce-scatter.2.cloned.1.call-start
  7.2 0.7 slice.22
  7.9 5.1 %collective-permute-start = (bf16[2,1,2048]{2,0,1:T(2,128)(2,1)S(1)}, bf16[2,1,2048]{2,0,1:T(2,128)(2,1)S(1)}, u32[]{:S(2)}, u32[]{:S(2)}) collective-permute-start(bf16[2,1,2048]{2,0,1:T(2,128)(2,1)S(1)} %slice.22), channel_id=1, source_target_pairs={{1,0},{2,1},{3,2},{4,3},{5,4},{6,5},{7,6},{9,8},{10,9},{11,10},{12... | collective-permute-start | bytes 24584 | tf_op jit(solution)/shard_map/ppermute | solution.py:23
  13.1 0.1 sine_multiply_fusion
  14.5 0.0 collective-permute-done
  14.5 13.3 %fusion.17 = bf16[1,2,524288]{2,1,0:T(2,128)(2,1)S(1)} fusion(s32[]{:T(128)} %bitcast.2, bf16[2,1,2048]{2,0,1:T(2,128)(2,1)S(1)} %collective-permute-done, bf16[2,1,524288]{2,0,1:T(2,128)(2,1)} %param.3), kind=kLoop, calls=%fused_computation.47 | loop fusion | flops 4194304 | bytes 4202500 | tf_op jit(solution)/shard_map/vmap()/gather | solution.py:111
  27.8 23.8 %fusion.9 = (f32[524288]{0:T(1024)}, f32[524288]{0:T(1024)}) fusion(bf16[1,2,524288]{2,1,0:T(2,128)(2,1)S(1)} %fusion.17), kind=kLoop, calls=%fused_computation.24 | loop fusion | flops 1048576 | bytes 6291456 | tf_op jit(solution)/shard_map/convert_element_type | solution.py:118
  51.6 1.9 reshape.274
  53.5 2.9 %reshape.275 = f32[128,16,256]{2,1,0:T(8,128)} reshape(f32[524288]{0:T(1024)} %get-tuple-element.23) | data formatting | bytes 4194304 | tf_op jit(solution)/shard_map/convert_element_type | solution.py:118
  56.3 13.2 %add_convert_fusion.1 = (bf16[128,16,256]{2,1,0:T(8,128)(2,1)S(1)}, bf16[128,16,256]{2,1,0:T(8,128)(2,1)S(1)}) fusion(f32[128,16,256]{2,1,0:T(8,128)} %reshape.275, f32[128,16,256]{2,1,0:T(8,128)S(1)} %reshape.274, s32[]{:T(128)S(6)} %mul.318, s32[]{:T(128)} %bitcast.98), kind=kLoop, calls=%fused_computation.42 | loop fusion | flops 31457280 | bytes 6291464 | tf_op jit(solution)/shard_map/convert_element_type | solution.py:61
  69.5 0.5 fusion.60
  70.0 0.5 fusion.62
  70.5 0.5 convolution_subtract_fusion
  71.0 0.8 fusion.21
  71.8 1.7 fusion.28
  73.6 1.8 fusion.24
  75.3 1.8 fusion.18
  77.1 0.7 copy.50
  77.8 1.8 fusion.19
  79.7 0.7 copy.53
  80.4 0.2 pad_maximum_fusion.1
  80.6 17.8 %copy.54 = bf16[2,1,128,4096]{2,0,1,3:T(2,128)(2,1)S(1)} copy(bf16[2,1,128,4096]{2,3,1,0:T(8,128)(2,1)S(1)} %pad_maximum_fusion.1) | data formatting | bytes 4194304 | tf_op jit(solution)/shard_map/stack | solution.py:86
  98.4 60.2 %all_to_all.15 = bf16[2,1,128,4096]{2,0,1,3:T(2,128)(2,1)S(1)} all-to-all(bf16[2,1,128,4096]{2,0,1,3:T(2,128)(2,1)S(1)} %copy.54), channel_id=1, replica_groups=mesh['stn'=32,'tm'=8] {'stn'}, dimensions={3} | all-to-all | bytes 4194304 | tf_op jit(solution)/shard_map/all_to_all | solution.py:121
  158.6 1.4 copy.73
  160.0 0.7 fusion.31
  160.6 0.7 fusion.30
  161.3 0.7 add_bitcast_fusion
  162.0 0.7 subtract_bitcast_fusion
  162.6 2.4 %pad_maximum_fusion = f32[2,32,32,128]{1,2,3,0:T(8,128)} fusion(f32[1,32,32,128]{1,2,3,0:T(8,128)S(1)} %subtract_bitcast_fusion, f32[1,32,32,128]{1,2,3,0:T(8,128)S(1)} %add_bitcast_fusion), kind=kLoop, calls=%fused_computation | loop fusion | flops 262144 | bytes 2097152 | tf_op jit(solution)/shard_map/stack | solution.py:103
  165.1 4.8 %copy.57 = f32[2,32,32,128]{3,2,0,1:T(8,128)} copy(f32[2,32,32,128]{1,2,3,0:T(8,128)} %pad_maximum_fusion) | data formatting | bytes 2097152 | tf_op jit(solution)/shard_map/stack | solution.py:103
  169.9 0.0 reduce-scatter.2.cloned.1.call-update
  169.9 0.1 broadcast_subtract_fusion
  170.0 0.1 fusion.66
  170.1 29.1 %reduce-scatter.2.cloned.1.call-done = f32[2,4,32,128]{3,2,0,1:T(8,128)} async-done(((f32[2,32,32,128]{3,2,0,1:T(8,128)}), f32[2,4,32,128]{3,2,0,1:T(8,128)}) %reduce-scatter.2.cloned.1.call-update) | async-done | bytes 131088 | tf_op jit(solution)/shard_map/reduce_scatter | solution.py:122
  199.2 1.0 multiply_multiply_fusion
  200.2 0.7 copy.59
  200.9 0.9 fusion.45
  201.8 0.1 copy.63
  201.9 0.7 copy.60
  (2 shorter events, 0.0 us)
Async XLA Ops:
  7.2 192.1 %reduce-scatter.2.cloned.1.call-start = ((), (), s32[]{:S(2)}) async-start(), calls=%async_computation.2 | async-start | bytes 1179648 | tf_op jit(solution)/shard_map/reduce_scatter | solution.py:122
  7.9 6.5 %collective-permute-start = (bf16[2,1,2048]{2,0,1:T(2,128)(2,1)S(1)}, bf16[2,1,2048]{2,0,1:T(2,128)(2,1)S(1)}, u32[]{:S(2)}, u32[]{:S(2)}) collective-permute-start(bf16[2,1,2048]{2,0,1:T(2,128)(2,1)S(1)} %slice.22), channel_id=1, source_target_pairs={{1,0},{2,1},{3,2},{4,3},{5,4},{6,5},{7,6},{9,8},{10,9},{11,10},{12... | collective-permute-start | bytes 24584 | tf_op jit(solution)/shard_map/ppermute | solution.py:23
Sparse Core Ops, SparseCore 0:
  170.0 29.1 reduce-scatter.1
where the time goes:
time: 211 us; the launch traced here: 209 us
  blocking collectives  60.2 us (29%)
  other arithmetic  55.1 us (26%)
  local copies, waits for them, and re-layouts  32.3 us (15%)
  waiting for transfers between devices  29.2 us (14%)
  between operations  15.5 us (7%)
  matrix products  12.1 us (6%)
  starting transfers between devices  5.17 us (2%)
    all_to_all x1, blocking collectives, per_device(): lax.all_to_all(spectra, 'stn', split_axis=3, concat_axis=1, tiled=True)  60.2 us
    reduce_scatter x1, waiting for transfers between devices, per_device(): lax.psum_scatter(correlate(owned), 'tm', scatter_dimension=1, tiled=True)  29.1 us
    convert_element_type x1, other arithmetic, per_device(): pieces[1].astype(jnp.float32)  23.8 us
    another operation x1, local copies, waits for them, and re-layouts, channelize(): jnp.stack([spec_real.reshape(stations, frames, NCH).astype(jnp.bfloat16),...  17.8 us
    gather x1, other arithmetic, per_device(): lax.dynamic_slice_in_dim(stream_row, shift_by, slice_len, 1)  13.3 us
    convert_element_type x1, other arithmetic, rotate(): real_out = (real_in * cosine + imag_in * sine).astype(jnp.bfloat16)  13.2 us
    dot_general x4, matrix products, second_section(): jnp.einsum('sfkn,nm->sfmk', data, table, preferred_element_type=jnp.float32)  7.15 us
    ppermute x1, starting transfers between devices, from_behind(): return lax.ppermute(array, axis, pairs)  5.14 us
  transfers between devices with their start and end apart: 2, of which 1 were waited for; matrix products, arithmetic and copies ran while one was open for 0% of the time, Pallas kernels for 0%

commit v1 on v0

v1 whole, which is shorter than its diff:
```python
import functools
import math

import jax
import jax.numpy as jnp
from jax import lax
from jax.experimental import pallas as pl
from jax.experimental.pallas import tpu as pltpu
from jax.sharding import PartitionSpec as P

MESH = pl.DeviceIdType.MESH

LANES = 128
FIRST = 32
FRAMES_DEV = 128
STATIONS = 32
N_TM = 8
ROWS = 2 * FIRST * FRAMES_DEV
HALO = 32
TURN = 20
CHUNKS = (4, 4, 4, 4)
PAIRS = FIRST // 2
SIN = (1.0, -1 / 6, 1 / 120, -1 / 5040, 1 / 362880, -1 / 39916800, 1 / 6227020800)


def iota(shape, axis):
    return lax.broadcasted_iota(jnp.int32, shape, axis)


def cos_turns(phase):
    wrapped = phase & ((1 << TURN) - 1)
    folded = jnp.abs(wrapped - (1 << (TURN - 1)))
    w = (folded - (1 << (TURN - 2))).astype(jnp.float32) * (2.0 * math.pi / (1 << TURN))
    square = w * w
    total = jnp.full_like(w, SIN[-1])
    for coefficient in SIN[-2::-1]:
        total = total * square + coefficient
    return total * w


def sin_turns(phase):
    return cos_turns(phase - (1 << (TURN - 2)))


def nt_dot(left, right):
    return lax.dot_general(left, right, (((1,), (1,)), ((), ())), preferred_element_type=jnp.float32)


def kernel(
    delay_ref, rate_ref, x_ref, vis_ref, auto_ref,
    xb, first_ref, second_ref, perm_ref, twid_ref, frame_ref, turned_ref,
    tx, rx, rs_tx, rs_rx, acc_ref,
    load_sem, halo_sems, tx_sems, rx_sems, rs_tx_sems, rs_rx_sems,
):
    me = lax.axis_index("stn")
    tm = lax.axis_index("tm")
    barrier = pltpu.get_barrier_semaphore()

    def greet_stn(k, carry):
        pl.semaphore_signal(barrier, inc=1, device_id={"stn": lax.rem(me + k, STATIONS)}, device_id_type=MESH)
        return carry

    def greet_tm(k, carry):
        pl.semaphore_signal(barrier, inc=1, device_id={"tm": lax.rem(tm + k, N_TM)}, device_id_type=MESH)
        return carry

    lax.fori_loop(1, STATIONS, greet_stn, 0)
    lax.fori_loop(1, N_TM, greet_tm, 0)

    load = pltpu.make_async_copy(x_ref, xb.at[pl.ds(0, ROWS)], load_sem)
    load.start()
    xb[pl.ds(ROWS + HALO, 128 - HALO), :] = jnp.zeros((128 - HALO, LANES), jnp.bfloat16)

    @pl.when(tm == N_TM - 1)
    def _():
        xb[pl.ds(ROWS, HALO), :] = jnp.zeros((HALO, LANES), jnp.bfloat16)

    delay = delay_ref[0]
    rate = rate_ref[0]
    whole = delay >> 7
    part = delay & (LANES - 1)

    rows = iota((2 * FIRST, LANES), 0)
    lanes = iota((2 * FIRST, LANES), 1)
    k1 = rows & (FIRST - 1)
    for extra in range(2):
        shift = 2 * (whole + extra)
        j = ((lanes - shift) & 63) >> 1
        comp_in = lanes & 1
        comp_out = rows >> 5
        quarter = (comp_out - comp_in) * (1 << (TURN - 2))
        base = cos_turns(k1 * j * (1 << 15) + rate * 128 * j + quarter)
        base = base.reshape(2 * FIRST, 1, LANES)
        frame = iota((1, 8, LANES), 1)
        lane = iota((1, 8, LANES), 2)
        for v in range(5):
            hit = ((lane + (128 * v - shift)) >> 6) == frame
            block = jnp.where(hit, base, 0.0).reshape(2 * FIRST * 8, LANES)
            first_ref[:, pl.ds(extra * 640 + v * 128, 128)] = block.astype(jnp.bfloat16)

    k1 = iota((FIRST, LANES), 0)
    sample = (iota((FIRST, LANES), 1) - part) & (LANES - 1)
    phase = sample * k1 * 256 + rate * sample
    scale = 1.0 / 64.0
    twid_ref[0] = cos_turns(phase) * scale
    twid_ref[1] = sin_turns(phase) * scale
    start = tm * (FRAMES_DEV * 4096) + iota((FRAMES_DEV, LANES), 0) * 4096
    phase = rate * start
    frame_ref[0] = cos_turns(phase)
    frame_ref[1] = sin_turns(phase)

    row = iota((256, LANES), 0)
    sample = (iota((256, LANES), 1) - part) & (LANES - 1)
    k2 = (row >> 3) * 4 + (row & 3)
    phase = sample * k2 * (1 << 13)
    comp_out = (row >> 2) & 1
    for comp_in in range(2):
        quarter = (comp_out - comp_in) * (1 << (TURN - 2))
        second_ref[:, pl.ds(comp_in * LANES, LANES)] = cos_turns(phase + quarter).astype(jnp.bfloat16)

    out_row = iota((256, 256), 0)
    in_row = iota((256, 256), 1)
    channel = out_row >> 5
    source = (out_row & 15) * 16 + (channel >> 2) * 8 + ((out_row >> 4) & 1) * 4 + (channel & 3)
    perm_ref[...] = jnp.where(in_row == source, 1.0, 0.0).astype(jnp.bfloat16)

    pl.semaphore_wait(barrier, STATIONS - 1 + N_TM - 1)

    def halo(target):
        return pltpu.make_async_remote_copy(
            src_ref=x_ref.at[pl.ds(0, HALO)],
            dst_ref=xb.at[pl.ds(ROWS, HALO)],
            send_sem=halo_sems.at[0],
            recv_sem=halo_sems.at[1],
            device_id={"tm": target},
            device_id_type=MESH,
        )

    @pl.when(tm > 0)
    def _():
        halo(tm - 1).start()

    load.wait()

    lane_of = iota((1, 2 * LANES), 1) & (LANES - 1)
    upper = jnp.where(lane_of >= part, 1.0, 0.0).astype(jnp.bfloat16)
    lower = jnp.where(lane_of < part, 1.0, 0.0).astype(jnp.bfloat16)

    def first_stage(group, carry):
        base = pl.multiple_of(group * 1024, 1024)
        data = jnp.concatenate([xb[pl.ds(base, 640), :], xb[pl.ds(base + 512, 640), :]], axis=1)
        partial = jnp.dot(first_ref[:, pl.ds(0, 640)], data * upper, preferred_element_type=jnp.float32)
        partial += jnp.dot(first_ref[:, pl.ds(640, 640)], data * lower, preferred_element_type=jnp.float32)
        tc = twid_ref[0].reshape(FIRST, 1, LANES)
        ts = twid_ref[1].reshape(FIRST, 1, LANES)
        parts = []
        for half in range(2):
            at = pl.multiple_of(group * 16 + half * 8, 8)
            pc = frame_ref[0, pl.ds(at, 8), :].reshape(1, 8, LANES)
            ps = frame_ref[1, pl.ds(at, 8), :].reshape(1, 8, LANES)
            wc = tc * pc - ts * ps
            ws = ts * pc + tc * ps
            real = partial[:256, half * 128 : half * 128 + 128].reshape(FIRST, 8, LANES)
            imag = partial[256:, half * 128 : half * 128 + 128].reshape(FIRST, 8, LANES)
            parts.append((real * wc + imag * ws, imag * wc - real * ws))
        at = pl.multiple_of(group * 16, 16)
        for comp in range(2):
            both = jnp.concatenate([parts[0][comp], parts[1][comp]], axis=1)
            turned_ref[:, pl.ds(at, 16), pl.ds(comp * 128, 128)] = both.astype(jnp.bfloat16)
        return carry

    lax.fori_loop(0, 7, first_stage, 0)

    @pl.when(tm < N_TM - 1)
    def _():
        halo(tm).wait_recv()

    first_stage(7, 0)

    def second_stage(kp, carry):
        data = turned_ref[pl.ds(2 * kp, 2)].reshape(256, 256)
        spec = nt_dot(second_ref[...], data)
        even = spec[:, :128].reshape(32, 8, 128)
        odd = spec[:, 128:].reshape(32, 8, 128)
        tx[:, kp] = jnp.concatenate([even, odd], axis=1).astype(jnp.bfloat16)
        return carry

    def to_owner(at, count, index, owner):
        return pltpu.make_async_remote_copy(
            src_ref=tx.at[owner, pl.ds(at, count)],
            dst_ref=rx.at[me, pl.ds(at, count)],
            send_sem=tx_sems.at[index],
            recv_sem=rx_sems.at[index],
            device_id={"stn": owner},
            device_id_type=MESH,
        )

    def to_row_owner(at, count, index, owner):
        return pltpu.make_async_remote_copy(
            src_ref=rs_tx.at[owner, pl.ds(at, count)],
            dst_ref=rs_rx.at[tm, pl.ds(at, count)],
            send_sem=rs_tx_sems.at[index],
            recv_sem=rs_rx_sems.at[index],
            device_id={"tm": owner},
            device_id_type=MESH,
        )

    starts = [sum(CHUNKS[:i]) for i in range(len(CHUNKS))]
    for index, (at, count) in enumerate(zip(starts, CHUNKS)):
        lax.fori_loop(at, at + count, second_stage, 0)

        def send(k, carry, at=at, count=count, index=index):
            to_owner(at, count, index, lax.rem(me + k, STATIONS)).start()
            return carry

        lax.fori_loop(1, STATIONS, send, 0)
        pltpu.make_async_copy(
            tx.at[me, pl.ds(at, count)], rx.at[me, pl.ds(at, count)], rx_sems.at[index]
        ).start()

    lane_group = iota((1, LANES), 1) >> 5
    low_rows = iota((1, 8, LANES), 1) < 4

    def correlate(pair, carry):
        halves = []
        for half in range(2):
            data = [rx[pl.ds(16 * half, 16), 2 * pair + i].reshape(256, LANES) for i in range(2)]
            moved = jnp.dot(perm_ref[...], jnp.concatenate(data, axis=1), preferred_element_type=jnp.float32)
            halves.append(moved.astype(jnp.bfloat16).reshape(8, 2, 16, 256))
        for i in range(2):
            cut = slice(128 * i, 128 * i + 128)
            real = jnp.concatenate([halves[0][:, 0, :, cut], halves[1][:, 0, :, cut]], axis=1)
            imag = jnp.concatenate([halves[0][:, 1, :, cut], halves[1][:, 1, :, cut]], axis=1)
            plain = jnp.concatenate([real, imag], axis=2)
            crossed = jnp.concatenate([imag, -real], axis=2)
            both = jnp.concatenate([plain, crossed], axis=1)
            for quad in range(2):
                right = plain[4 * quad : 4 * quad + 4].reshape(128, 256)
                left = both[4 * quad : 4 * quad + 4].reshape(256, 256)
                product = nt_dot(left, right).reshape(4, 64, LANES)
                kept = product[0]
                for e in range(1, 4):
                    kept = jnp.where(lane_group == e, product[e], kept)
                kept = kept.reshape(2, 4, 8, LANES)
                turned = pltpu.roll(kept.reshape(8, 8, LANES), 4, 1).reshape(2, 4, 8, LANES)
                even = jnp.where(low_rows, kept[0], turned[1])
                odd = jnp.where(low_rows, turned[0], kept[1])
                mixed = jnp.concatenate([even.reshape(4, 1, 8, LANES), odd.reshape(4, 1, 8, LANES)], axis=1)
                rs_tx[:, 2 * pair + i, quad] = mixed.reshape(N_TM, 8, LANES)
        return carry

    for index, (at, count) in enumerate(zip(starts, CHUNKS)):
        arrived = rx.at[:, pl.ds(at, count)]
        pltpu.make_async_copy(arrived, arrived, rx_sems.at[index]).wait()
        lax.fori_loop(at // 2, (at + count) // 2, correlate, 0)

        def send(k, carry, at=at, count=count, index=index):
            to_row_owner(at, count, index, lax.rem(tm + k, N_TM)).start()
            return carry

        lax.fori_loop(1, N_TM, send, 0)
        pltpu.make_async_copy(
            rs_tx.at[tm, pl.ds(at, count)], rs_rx.at[tm, pl.ds(at, count)], rs_rx_sems.at[index]
        ).start()

    for index, (at, count) in enumerate(zip(starts, CHUNKS)):
        arrived = rs_rx.at[:, pl.ds(at, count)]
        pltpu.make_async_copy(arrived, arrived, rs_rx_sems.at[index]).wait()
        total = rs_rx[0, pl.ds(at, count)]
        for source in range(1, N_TM):
            total = total + rs_rx[source, pl.ds(at, count)]
        acc_ref[pl.ds(2 * at, 2 * count)] = total.reshape(2 * count, 8, LANES)

    lane_group = iota((32, LANES), 1) >> 5
    station = iota((32, LANES), 0)
    for comp in range(2):
        stacked = jnp.concatenate([acc_ref[:, 4 * comp + r, :] for r in range(4)], axis=0)
        flipped = stacked.T.reshape(4, 32, LANES)
        for r in range(4):
            block = jnp.zeros((32, LANES), jnp.float32)
            for k2 in range(4):
                shift = (32 * (k2 - r)) % 128
                piece = flipped[k2] if shift == 0 else pltpu.roll(flipped[k2], shift, 1)
                block = jnp.where(lane_group == k2, piece, block)
            diagonal = station == 4 * tm + r
            vis_ref[4 * comp + r] = jnp.where(diagonal, 0.0, block * (1.0 / 32.0))
            if comp == 0:
                own = jnp.sum(jnp.where(diagonal, block, 0.0), axis=0, keepdims=True)
                auto_ref[pl.ds(r, 1), :] = own * (1.0 / 1024.0)

    for index, (at, count) in enumerate(zip(starts, CHUNKS)):
        sent = tx.at[pl.ds(0, STATIONS - 1), pl.ds(at, count)]
        pltpu.make_async_copy(sent, sent, tx_sems.at[index]).wait()
        sent = rs_tx.at[pl.ds(0, N_TM - 1), pl.ds(at, count)]
        pltpu.make_async_copy(sent, sent, rs_tx_sems.at[index]).wait()

    @pl.when(tm > 0)
    def _():
        halo(tm).wait_send()


def per_device(streams, sample_delays, fringe_rates):
    data = streams.reshape(2, ROWS // 2, LANES).transpose(1, 0, 2).reshape(ROWS, LANES)
    chunks = len(CHUNKS)
    vis, auto = pl.pallas_call(
        kernel,
        out_shape=(
            jax.ShapeDtypeStruct((8, STATIONS, LANES), jnp.float32),
            jax.ShapeDtypeStruct((4, LANES), jnp.float32),
        ),
        in_specs=[
            pl.BlockSpec(memory_space=pltpu.SMEM),
            pl.BlockSpec(memory_space=pltpu.SMEM),
            pl.BlockSpec(memory_space=pl.ANY),
        ],
        out_specs=(pl.BlockSpec(memory_space=pltpu.VMEM), pl.BlockSpec(memory_space=pltpu.VMEM)),
        scratch_shapes=[
            pltpu.VMEM((ROWS + 128, LANES), jnp.bfloat16),
            pltpu.VMEM((512, 1280), jnp.bfloat16),
            pltpu.VMEM((256, 256), jnp.bfloat16),
            pltpu.VMEM((256, 256), jnp.bfloat16),
            pltpu.VMEM((2, FIRST, LANES), jnp.float32),
            pltpu.VMEM((2, FRAMES_DEV, LANES), jnp.float32),
            pltpu.VMEM((FIRST, FRAMES_DEV, 256), jnp.bfloat16),
            pltpu.VMEM((STATIONS, PAIRS, 16, LANES), jnp.bfloat16),
            pltpu.VMEM((STATIONS, PAIRS, 16, LANES), jnp.bfloat16),
            pltpu.VMEM((N_TM, PAIRS, 2, 8, LANES), jnp.float32),
            pltpu.VMEM((N_TM, PAIRS, 2, 8, LANES), jnp.float32),
            pltpu.VMEM((FIRST, 8, LANES), jnp.float32),
            pltpu.SemaphoreType.DMA,
            pltpu.SemaphoreType.DMA((2,)),
            pltpu.SemaphoreType.DMA((chunks,)),
            pltpu.SemaphoreType.DMA((chunks,)),
            pltpu.SemaphoreType.DMA((chunks,)),
            pltpu.SemaphoreType.DMA((chunks,)),
        ],
        compiler_params=pltpu.CompilerParams(
            collective_id=0, has_side_effects=True, vmem_limit_bytes=48 << 20
        ),
    )(sample_delays, fringe_rates, data)
    return vis.reshape(2, 4, STATIONS, LANES), auto


def solution(mesh):
    in_specs = (P(None, "stn", "tm"), P("stn"), P("stn"))
    out_specs = (P(None, "tm", None, "stn"), P("tm", "stn"))
    return jax.shard_map(
        per_device, mesh=mesh, in_specs=in_specs, out_specs=out_specs, check_vma=False
    )
```

time: 211 us -> 75.5 us (0.36)
  Pallas kernels: 0 us -> 70.6 us
  blocking collectives: 60.2 us -> 0 us
  other arithmetic: 55.1 us -> 0 us
  local copies, waits for them, and re-layouts: 32.3 us -> 2.82 us
  waiting for transfers between devices: 29.2 us -> 0 us
  between operations: 15.5 us -> 1.94 us
  matrix products: 12.1 us -> 0 us
  starting transfers between devices: 5.17 us -> 0 us
    pallas_call x0 -> x1, Pallas kernels: none -> 70.6 us  [per_device(): pl.pallas_call(kernel, out_shape=(jax.ShapeDtypeStruct((8, STATIONS, LANE...]
    all_to_all x1 -> x0, blocking collectives: 60.2 us -> none  [per_device(): lax.all_to_all(spectra, 'stn', split_axis=3, concat_axis=1, tiled=True)]
    convert_element_type x3 -> x0, other arithmetic: 37.1 us -> none  [the longest x1 23.8 us: per_device(): pieces[1].astype(jnp.float32)]
    reduce_scatter x1 -> x0, waiting for transfers between devices: 29.1 us -> none  [per_device(): lax.psum_scatter(correlate(owned), 'tm', scatter_dimension=1, tiled=True)]
    another operation x2 -> x0, local copies, waits for them, and re-layouts: 22.7 us -> none  [the longest x1 17.8 us: channelize(): jnp.stack([spec_real.reshape(stations, frames, NCH).astype(jnp.bfloat16),...]
    gather x1 -> x0, other arithmetic: 13.3 us -> none  [per_device(): lax.dynamic_slice_in_dim(stream_row, shift_by, slice_len, 1)]
    dot_general x12 -> x0, matrix products: 12.1 us -> none  [the longest x4 7.15 us: second_section(): jnp.einsum('sfkn,nm->sfmk', data, table, preferred_element_type=jnp.float32)]
    convert_element_type x4 -> x0, local copies, waits for them, and re-layouts: 6.1 us -> none  [the longest x1 2.85 us: per_device(): pieces[1].astype(jnp.float32)]
  transfers between devices with their start and end apart: 2 -> 0, of which waited for: 1 -> 0; matrix products, arithmetic and copies ran while one was open for 0% -> 0% of each run, Pallas kernels for 0% -> 0%
where the time goes in v1:
time: 75.5 us; the launch traced here: 75.4 us
  Pallas kernels  70.6 us (94%)
  local copies, waits for them, and re-layouts  2.82 us (4%)
  between operations  1.94 us (3%)
    pallas_call x1, Pallas kernels, per_device(): pl.pallas_call(kernel, out_shape=(jax.ShapeDtypeStruct((8, STATIONS, LANE...  70.6 us
    unnamed x4, local copies, waits for them, and re-layouts  2.82 us

profile of v1, /device:TPU:1, one launch (start us, length us, event | category | flops | bytes accessed | tf_op | source)
XLA Modules:
  0.0 75.4 jit_solution(11474192270367662931)
XLA Ops:
  1.9 0.0 copy-start
  1.9 1.6 %copy-done = bf16[2,1,524288]{2,0,1:T(2,128)(2,1)S(1)} copy-done((bf16[2,1,524288]{2,0,1:T(2,128)(2,1)S(1)}, bf16[2,1,524288]{2,0,1:T(2,128)(2,1)}, u32[]{:S(2)}) %copy-start) | copy-done | bytes 2097176
  3.5 70.6 %shard_map.50 = (f32[8,32,128]{2,1,0:T(8,128)S(1)}, f32[4,128]{1,0:T(4,128)S(1)}) custom-call(s32[1]{0:T(128)S(6)} %copy.8.delay_ref, s32[1]{0:T(128)S(6)} %copy.9.rate_ref, bf16[8192,128]{1,0:T(8,128)(2,1)S(1)} %bitcast.6), custom_call_target="tpu_custom_call" | custom-call | tf_op jit(solution)/shard_map/pallas_call | solution.py:305
  74.1 0.7 copy.10
  74.8 0.6 copy.11
Async XLA Ops:
  1.9 1.6 %copy-start = (bf16[2,1,524288]{2,0,1:T(2,128)(2,1)S(1)}, bf16[2,1,524288]{2,0,1:T(2,128)(2,1)}, u32[]{:S(2)}) copy-start(bf16[2,1,524288]{2,0,1:T(2,128)(2,1)} %param.3) | copy-start | bytes 6291460

commit v2 on v1

--- a/solution.py
+++ b/solution.py
@@ -18,7 +18,7 @@
 ROWS = 2 * FIRST * FRAMES_DEV
 HALO = 32
 TURN = 20
-CHUNKS = (4, 4, 4, 4)
+CHUNKS = (2, 4, 4, 3, 2, 1)
 PAIRS = FIRST // 2
 SIN = (1.0, -1 / 6, 1 / 120, -1 / 5040, 1 / 362880, -1 / 39916800, 1 / 6227020800)
 
@@ -47,10 +47,10 @@
 
 
 def kernel(
-    delay_ref, rate_ref, x_ref, vis_ref, auto_ref,
-    xb, first_ref, second_ref, perm_ref, twid_ref, frame_ref, turned_ref,
-    tx, rx, rs_tx, rs_rx, acc_ref,
-    load_sem, halo_sems, tx_sems, rx_sems, rs_tx_sems, rs_rx_sems,
+    delay_hbm, rate_hbm, x_ref, acc_ref,
+    delay_ref, rate_ref, xb, first_ref, second_ref, perm_ref, twid_ref, frame_ref, turned_ref,
+    tx, rx, rs_tx, rs_rx,
+    scalar_sems, load_sems, halo_sems, tx_sems, rx_sems, rs_tx_sems, rs_rx_sems,
 ):
     me = lax.axis_index("stn")
     tm = lax.axis_index("tm")
@@ -64,17 +64,29 @@
         pl.semaphore_signal(barrier, inc=1, device_id={"tm": lax.rem(tm + k, N_TM)}, device_id_type=MESH)
         return carry
 
+    def load(piece):
+        at = pl.multiple_of(piece * 1024, 1024)
+        return pltpu.make_async_copy(x_ref.at[pl.ds(at, 1024)], xb.at[pl.ds(at, 1024)], load_sems.at[piece])
+
+    scalars = [
+        pltpu.make_async_copy(source, target, scalar_sems.at[i])
+        for i, (source, target) in enumerate(((delay_hbm, delay_ref), (rate_hbm, rate_ref)))
+    ]
+    for copy in scalars:
+        copy.start()
+    for piece in range(8):
+        load(piece).start()
     lax.fori_loop(1, STATIONS, greet_stn, 0)
     lax.fori_loop(1, N_TM, greet_tm, 0)
 
-    load = pltpu.make_async_copy(x_ref, xb.at[pl.ds(0, ROWS)], load_sem)
-    load.start()
     xb[pl.ds(ROWS + HALO, 128 - HALO), :] = jnp.zeros((128 - HALO, LANES), jnp.bfloat16)
 
     @pl.when(tm == N_TM - 1)
     def _():
         xb[pl.ds(ROWS, HALO), :] = jnp.zeros((HALO, LANES), jnp.bfloat16)
 
+    for copy in scalars:
+        copy.wait()
     delay = delay_ref[0]
     rate = rate_ref[0]
     whole = delay >> 7
@@ -124,8 +136,6 @@
     source = (out_row & 15) * 16 + (channel >> 2) * 8 + ((out_row >> 4) & 1) * 4 + (channel & 3)
     perm_ref[...] = jnp.where(in_row == source, 1.0, 0.0).astype(jnp.bfloat16)
 
-    pl.semaphore_wait(barrier, STATIONS - 1 + N_TM - 1)
-
     def halo(target):
         return pltpu.make_async_remote_copy(
             src_ref=x_ref.at[pl.ds(0, HALO)],
@@ -136,23 +146,21 @@
             device_id_type=MESH,
         )
 
-    @pl.when(tm > 0)
-    def _():
-        halo(tm - 1).start()
-
-    load.wait()
-
     lane_of = iota((1, 2 * LANES), 1) & (LANES - 1)
     upper = jnp.where(lane_of >= part, 1.0, 0.0).astype(jnp.bfloat16)
     lower = jnp.where(lane_of < part, 1.0, 0.0).astype(jnp.bfloat16)
 
-    def first_stage(group, carry):
+    def first_stage(group, low, high):
+        count = high - low
         base = pl.multiple_of(group * 1024, 1024)
         data = jnp.concatenate([xb[pl.ds(base, 640), :], xb[pl.ds(base + 512, 640), :]], axis=1)
-        partial = jnp.dot(first_ref[:, pl.ds(0, 640)], data * upper, preferred_element_type=jnp.float32)
-        partial += jnp.dot(first_ref[:, pl.ds(640, 640)], data * lower, preferred_element_type=jnp.float32)
-        tc = twid_ref[0].reshape(FIRST, 1, LANES)
-        ts = twid_ref[1].reshape(FIRST, 1, LANES)
+        data = jnp.concatenate([data * upper, data * lower], axis=0)
+        partial = [
+            jnp.dot(first_ref[pl.ds(comp * 256 + 8 * low, 8 * count)], data, preferred_element_type=jnp.float32)
+            for comp in range(2)
+        ]
+        tc = twid_ref[0, pl.ds(low, count)].reshape(count, 1, LANES)
+        ts = twid_ref[1, pl.ds(low, count)].reshape(count, 1, LANES)
         parts = []
         for half in range(2):
             at = pl.multiple_of(group * 16 + half * 8, 8)
@@ -160,22 +168,40 @@
             ps = frame_ref[1, pl.ds(at, 8), :].reshape(1, 8, LANES)
             wc = tc * pc - ts * ps
             ws = ts * pc + tc * ps
-            real = partial[:256, half * 128 : half * 128 + 128].reshape(FIRST, 8, LANES)
-            imag = partial[256:, half * 128 : half * 128 + 128].reshape(FIRST, 8, LANES)
+            real, imag = (p[:, half * 128 : half * 128 + 128].reshape(count, 8, LANES) for p in partial)
             parts.append((real * wc + imag * ws, imag * wc - real * ws))
         at = pl.multiple_of(group * 16, 16)
         for comp in range(2):
             both = jnp.concatenate([parts[0][comp], parts[1][comp]], axis=1)
-            turned_ref[:, pl.ds(at, 16), pl.ds(comp * 128, 128)] = both.astype(jnp.bfloat16)
-        return carry
-
-    lax.fori_loop(0, 7, first_stage, 0)
+            turned_ref[pl.ds(low, count), pl.ds(at, 16), pl.ds(comp * 128, 128)] = both.astype(jnp.bfloat16)
+
+    head = 2 * CHUNKS[0]
+
+    def head_group(group, carry):
+        load(group + 1).wait()
+        first_stage(group, 0, head)
+        return carry
+
+    def rest_group(group, carry):
+        first_stage(group, head, FIRST)
+        return carry
+
+    load(0).wait()
+    lax.fori_loop(0, 7, head_group, 0)
+
+    pl.semaphore_wait(barrier, STATIONS - 1 + N_TM - 1)
+
+    @pl.when(tm > 0)
+    def _():
+        halo(tm - 1).start()
+
+    lax.fori_loop(0, 3, rest_group, 0)
 
     @pl.when(tm < N_TM - 1)
     def _():
         halo(tm).wait_recv()
 
-    first_stage(7, 0)
+    first_stage(7, 0, head)
 
     def second_stage(kp, carry):
         data = turned_ref[pl.ds(2 * kp, 2)].reshape(256, 256)
@@ -207,6 +233,8 @@
 
     starts = [sum(CHUNKS[:i]) for i in range(len(CHUNKS))]
     for index, (at, count) in enumerate(zip(starts, CHUNKS)):
+        if index == 1:
+            lax.fori_loop(3, 8, rest_group, 0)
         lax.fori_loop(at, at + count, second_stage, 0)
 
         def send(k, carry, at=at, count=count, index=index):
@@ -221,13 +249,13 @@
     lane_group = iota((1, LANES), 1) >> 5
     low_rows = iota((1, 8, LANES), 1) < 4
 
-    def correlate(pair, carry):
+    def correlate(first, count):
         halves = []
         for half in range(2):
-            data = [rx[pl.ds(16 * half, 16), 2 * pair + i].reshape(256, LANES) for i in range(2)]
+            data = [rx[pl.ds(16 * half, 16), first + i].reshape(256, LANES) for i in range(count)]
             moved = jnp.dot(perm_ref[...], jnp.concatenate(data, axis=1), preferred_element_type=jnp.float32)
-            halves.append(moved.astype(jnp.bfloat16).reshape(8, 2, 16, 256))
-        for i in range(2):
+            halves.append(moved.astype(jnp.bfloat16).reshape(8, 2, 16, 128 * count))
+        for i in range(count):
             cut = slice(128 * i, 128 * i + 128)
             real = jnp.concatenate([halves[0][:, 0, :, cut], halves[1][:, 0, :, cut]], axis=1)
             imag = jnp.concatenate([halves[0][:, 1, :, cut], halves[1][:, 1, :, cut]], axis=1)
@@ -246,24 +274,11 @@
                 even = jnp.where(low_rows, kept[0], turned[1])
                 odd = jnp.where(low_rows, turned[0], kept[1])
                 mixed = jnp.concatenate([even.reshape(4, 1, 8, LANES), odd.reshape(4, 1, 8, LANES)], axis=1)
-                rs_tx[:, 2 * pair + i, quad] = mixed.reshape(N_TM, 8, LANES)
-        return carry
-
-    for index, (at, count) in enumerate(zip(starts, CHUNKS)):
-        arrived = rx.at[:, pl.ds(at, count)]
-        pltpu.make_async_copy(arrived, arrived, rx_sems.at[index]).wait()
-        lax.fori_loop(at // 2, (at + count) // 2, correlate, 0)
-
-        def send(k, carry, at=at, count=count, index=index):
-            to_row_owner(at, count, index, lax.rem(tm + k, N_TM)).start()
-            return carry
-
-        lax.fori_loop(1, N_TM, send, 0)
-        pltpu.make_async_copy(
-            rs_tx.at[tm, pl.ds(at, count)], rs_rx.at[tm, pl.ds(at, count)], rs_rx_sems.at[index]
-        ).start()
-
-    for index, (at, count) in enumerate(zip(starts, CHUNKS)):
+                rs_tx[:, first + i, quad] = mixed.reshape(N_TM, 8, LANES)
+
+
+    def gather_sums(index):
+        at, count = starts[index], CHUNKS[index]
         arrived = rs_rx.at[:, pl.ds(at, count)]
         pltpu.make_async_copy(arrived, arrived, rs_rx_sems.at[index]).wait()
         total = rs_rx[0, pl.ds(at, count)]
@@ -271,6 +286,44 @@
             total = total + rs_rx[source, pl.ds(at, count)]
         acc_ref[pl.ds(2 * at, 2 * count)] = total.reshape(2 * count, 8, LANES)
 
+    for index, (at, count) in enumerate(zip(starts, CHUNKS)):
+        arrived = rx.at[:, pl.ds(at, count)]
+        pltpu.make_async_copy(arrived, arrived, rx_sems.at[index]).wait()
+
+        def correlate_pair(pair, carry, at=at):
+            correlate(at + 2 * pair, 2)
+            return carry
+
+        lax.fori_loop(0, count // 2, correlate_pair, 0)
+        if count % 2:
+            correlate(at + count - 1, 1)
+
+        def send(k, carry, at=at, count=count, index=index):
+            to_row_owner(at, count, index, lax.rem(tm + k, N_TM)).start()
+            return carry
+
+        lax.fori_loop(1, N_TM, send, 0)
+        pltpu.make_async_copy(
+            rs_tx.at[tm, pl.ds(at, count)], rs_rx.at[tm, pl.ds(at, count)], rs_rx_sems.at[index]
+        ).start()
+        if index > 0:
+            gather_sums(index - 1)
+
+    gather_sums(len(CHUNKS) - 1)
+
+    for index, (at, count) in enumerate(zip(starts, CHUNKS)):
+        sent = tx.at[pl.ds(0, STATIONS - 1), pl.ds(at, count)]
+        pltpu.make_async_copy(sent, sent, tx_sems.at[index]).wait()
+        sent = rs_tx.at[pl.ds(0, N_TM - 1), pl.ds(at, count)]
+        pltpu.make_async_copy(sent, sent, rs_tx_sems.at[index]).wait()
+
+    @pl.when(tm > 0)
+    def _():
+        halo(tm).wait_send()
+
+
+def finish(acc_ref, vis_ref, auto_ref):
+    tm = lax.axis_index("tm")
     lane_group = iota((32, LANES), 1) >> 5
     station = iota((32, LANES), 0)
     for comp in range(2):
@@ -288,33 +341,18 @@
                 own = jnp.sum(jnp.where(diagonal, block, 0.0), axis=0, keepdims=True)
                 auto_ref[pl.ds(r, 1), :] = own * (1.0 / 1024.0)
 
-    for index, (at, count) in enumerate(zip(starts, CHUNKS)):
-        sent = tx.at[pl.ds(0, STATIONS - 1), pl.ds(at, count)]
-        pltpu.make_async_copy(sent, sent, tx_sems.at[index]).wait()
-        sent = rs_tx.at[pl.ds(0, N_TM - 1), pl.ds(at, count)]
-        pltpu.make_async_copy(sent, sent, rs_tx_sems.at[index]).wait()
-
-    @pl.when(tm > 0)
-    def _():
-        halo(tm).wait_send()
-
 
 def per_device(streams, sample_delays, fringe_rates):
     data = streams.reshape(2, ROWS // 2, LANES).transpose(1, 0, 2).reshape(ROWS, LANES)
     chunks = len(CHUNKS)
-    vis, auto = pl.pallas_call(
+    sums = pl.pallas_call(
         kernel,
-        out_shape=(
-            jax.ShapeDtypeStruct((8, STATIONS, LANES), jnp.float32),
-            jax.ShapeDtypeStruct((4, LANES), jnp.float32),
-        ),
-        in_specs=[
-            pl.BlockSpec(memory_space=pltpu.SMEM),
-            pl.BlockSpec(memory_space=pltpu.SMEM),
-            pl.BlockSpec(memory_space=pl.ANY),
-        ],
-        out_specs=(pl.BlockSpec(memory_space=pltpu.VMEM), pl.BlockSpec(memory_space=pltpu.VMEM)),
+        out_shape=jax.ShapeDtypeStruct((FIRST, 8, LANES), jnp.float32),
+        in_specs=[pl.BlockSpec(memory_space=pltpu.HBM)] * 3,
+        out_specs=pl.BlockSpec(memory_space=pltpu.VMEM),
         scratch_shapes=[
+            pltpu.SMEM((1,), jnp.int32),
+            pltpu.SMEM((1,), jnp.int32),
             pltpu.VMEM((ROWS + 128, LANES), jnp.bfloat16),
             pltpu.VMEM((512, 1280), jnp.bfloat16),
             pltpu.VMEM((256, 256), jnp.bfloat16),
@@ -326,8 +364,8 @@
             pltpu.VMEM((STATIONS, PAIRS, 16, LANES), jnp.bfloat16),
             pltpu.VMEM((N_TM, PAIRS, 2, 8, LANES), jnp.float32),
             pltpu.VMEM((N_TM, PAIRS, 2, 8, LANES), jnp.float32),
-            pltpu.VMEM((FIRST, 8, LANES), jnp.float32),
-            pltpu.SemaphoreType.DMA,
+            pltpu.SemaphoreType.DMA((2,)),
+            pltpu.SemaphoreType.DMA((8,)),
             pltpu.SemaphoreType.DMA((2,)),
             pltpu.SemaphoreType.DMA((chunks,)),
             pltpu.SemaphoreType.DMA((chunks,)),
@@ -335,9 +373,17 @@
             pltpu.SemaphoreType.DMA((chunks,)),
         ],
         compiler_params=pltpu.CompilerParams(
-            collective_id=0, has_side_effects=True, vmem_limit_bytes=48 << 20
+            collective_id=0, has_side_effects=True, vmem_limit_bytes=52 << 20
         ),
     )(sample_delays, fringe_rates, data)
+    vis, auto = pl.pallas_call(
+        finish,
+        out_shape=(
+            jax.ShapeDtypeStruct((8, STATIONS, LANES), jnp.float32),
+            jax.ShapeDtypeStruct((4, LANES), jnp.float32),
+        ),
+        compiler_params=pltpu.CompilerParams(vmem_limit_bytes=4 << 20),
+    )(sums)
     return vis.reshape(2, 4, STATIONS, LANES), auto
 
 

time: 75.5 us -> 70.1 us (0.928)
  local copies, waits for them, and re-layouts: 2.82 us -> 0 us
  Pallas kernels: 70.6 us -> 68 us
    unnamed x4 -> x0, local copies, waits for them, and re-layouts: 2.82 us -> none
    pallas_call x1 -> x2, Pallas kernels: 70.6 us -> 68 us  [the longest x1 67.1 us: per_device(): pl.pallas_call(kernel, out_shape=jax.ShapeDtypeStruct((FIRST, 8, LANES),...]
where the time goes in v2:
time: 70.1 us; the launch traced here: 70 us
  Pallas kernels  68 us (97%)
  between operations  1.93 us (3%)
    pallas_call x1, Pallas kernels, per_device(): pl.pallas_call(kernel, out_shape=jax.ShapeDtypeStruct((FIRST, 8, LANES),...  67.1 us

profile of v2, /device:TPU:1, one launch (start us, length us, event | category | flops | bytes accessed | tf_op | source)
XLA Modules:
  0.0 70.0 jit_solution(17479032813709254371)
XLA Ops:
  1.9 67.1 %shard_map.50.acc_ref = f32[32,8,128]{2,1,0:T(8,128)S(1)} custom-call(s32[1]{0:T(128)S(6)} %copy.6.delay_hbm, s32[1]{0:T(128)S(6)} %copy.7.rate_hbm, bf16[8192,128]{1,0:T(8,128)(2,1)} %bitcast.6), custom_call_target="tpu_custom_call" | custom-call | tf_op jit(solution)/shard_map/pallas_call | solution.py:348
  69.0 1.0 %shard_map.51 = (f32[8,32,128]{2,1,0:T(8,128)}, f32[4,128]{1,0:T(4,128)}) custom-call(f32[32,8,128]{2,1,0:T(8,128)S(1)} %shard_map.50.acc_ref), custom_call_target="tpu_custom_call" | custom-call | tf_op jit(solution)/shard_map/pallas_call | solution.py:379

commit v3 on v2

--- a/solution.py
+++ b/solution.py
@@ -18,6 +18,7 @@
 ROWS = 2 * FIRST * FRAMES_DEV
 HALO = 32
 TURN = 20
+HEAD_ROWS = 544
 CHUNKS = (2, 4, 4, 3, 2, 1)
 PAIRS = FIRST // 2
 SIN = (1.0, -1 / 6, 1 / 120, -1 / 5040, 1 / 362880, -1 / 39916800, 1 / 6227020800)
@@ -76,8 +77,8 @@
         copy.start()
     for piece in range(8):
         load(piece).start()
-    lax.fori_loop(1, STATIONS, greet_stn, 0)
-    lax.fori_loop(1, N_TM, greet_tm, 0)
+    lax.fori_loop(1, STATIONS, greet_stn, 0, unroll=True)
+    lax.fori_loop(1, N_TM, greet_tm, 0, unroll=True)
 
     xb[pl.ds(ROWS + HALO, 128 - HALO), :] = jnp.zeros((128 - HALO, LANES), jnp.bfloat16)
 
@@ -148,17 +149,23 @@
 
     lane_of = iota((1, 2 * LANES), 1) & (LANES - 1)
     upper = jnp.where(lane_of >= part, 1.0, 0.0).astype(jnp.bfloat16)
+    wraps = lane_of < part
     lower = jnp.where(lane_of < part, 1.0, 0.0).astype(jnp.bfloat16)
 
     def first_stage(group, low, high):
         count = high - low
         base = pl.multiple_of(group * 1024, 1024)
         data = jnp.concatenate([xb[pl.ds(base, 640), :], xb[pl.ds(base + 512, 640), :]], axis=1)
-        data = jnp.concatenate([data * upper, data * lower], axis=0)
-        partial = [
-            jnp.dot(first_ref[pl.ds(comp * 256 + 8 * low, 8 * count)], data, preferred_element_type=jnp.float32)
-            for comp in range(2)
-        ]
+        rows = [pl.ds(comp * 256 + 8 * low, 8 * count) for comp in range(2)]
+        if low == 0:
+            data = data[:HEAD_ROWS]
+            table = [first_ref[rows[comp], pl.ds(640 * extra, HEAD_ROWS)] for extra in range(2) for comp in range(2)]
+            product = jnp.dot(jnp.concatenate(table, axis=0), data, preferred_element_type=jnp.float32)
+            product = product.reshape(4, 8 * count, 256)
+            partial = [jnp.where(wraps, product[2 + comp], product[comp]) for comp in range(2)]
+        else:
+            data = jnp.concatenate([data * upper, data * lower], axis=0)
+            partial = [jnp.dot(first_ref[rows[comp]], data, preferred_element_type=jnp.float32) for comp in range(2)]
         tc = twid_ref[0, pl.ds(low, count)].reshape(count, 1, LANES)
         ts = twid_ref[1, pl.ds(low, count)].reshape(count, 1, LANES)
         parts = []
@@ -195,21 +202,19 @@
     def _():
         halo(tm - 1).start()
 
-    lax.fori_loop(0, 3, rest_group, 0)
-
     @pl.when(tm < N_TM - 1)
     def _():
         halo(tm).wait_recv()
 
     first_stage(7, 0, head)
 
-    def second_stage(kp, carry):
-        data = turned_ref[pl.ds(2 * kp, 2)].reshape(256, 256)
+    def second_stage(first, count):
+        data = turned_ref[pl.ds(2 * first, 2 * count)].reshape(256 * count, 256)
         spec = nt_dot(second_ref[...], data)
-        even = spec[:, :128].reshape(32, 8, 128)
-        odd = spec[:, 128:].reshape(32, 8, 128)
-        tx[:, kp] = jnp.concatenate([even, odd], axis=1).astype(jnp.bfloat16)
-        return carry
+        for i in range(count):
+            even = spec[:, 256 * i : 256 * i + 128].reshape(32, 8, 128)
+            odd = spec[:, 256 * i + 128 : 256 * i + 256].reshape(32, 8, 128)
+            tx[:, first + i] = jnp.concatenate([even, odd], axis=1).astype(jnp.bfloat16)
 
     def to_owner(at, count, index, owner):
         return pltpu.make_async_remote_copy(
@@ -234,14 +239,21 @@
     starts = [sum(CHUNKS[:i]) for i in range(len(CHUNKS))]
     for index, (at, count) in enumerate(zip(starts, CHUNKS)):
         if index == 1:
-            lax.fori_loop(3, 8, rest_group, 0)
-        lax.fori_loop(at, at + count, second_stage, 0)
+            lax.fori_loop(0, 8, rest_group, 0)
+
+        def second_pair(pair, carry, at=at):
+            second_stage(at + 2 * pair, 2)
+            return carry
+
+        lax.fori_loop(0, count // 2, second_pair, 0)
+        if count % 2:
+            second_stage(at + count - 1, 1)
 
         def send(k, carry, at=at, count=count, index=index):
             to_owner(at, count, index, lax.rem(me + k, STATIONS)).start()
             return carry
 
-        lax.fori_loop(1, STATIONS, send, 0)
+        lax.fori_loop(1, STATIONS, send, 0, unroll=True)
         pltpu.make_async_copy(
             tx.at[me, pl.ds(at, count)], rx.at[me, pl.ds(at, count)], rx_sems.at[index]
         ).start()
@@ -302,7 +314,8 @@
             to_row_owner(at, count, index, lax.rem(tm + k, N_TM)).start()
             return carry
 
-        lax.fori_loop(1, N_TM, send, 0)
+        for k in (4, 5, 3, 6, 2, 7, 1):
+            send(k, 0)
         pltpu.make_async_copy(
             rs_tx.at[tm, pl.ds(at, count)], rs_rx.at[tm, pl.ds(at, count)], rs_rx_sems.at[index]
         ).start()

time: 70.1 us -> 67.6 us (0.964)
  Pallas kernels: 68 us -> 65.6 us
    pallas_call x1, Pallas kernels: 67.1 us -> 64.6 us  [per_device(): pl.pallas_call(kernel, out_shape=jax.ShapeDtypeStruct((FIRST, 8, LANES),...]
where the time goes in v3:
time: 67.6 us; the launch traced here: 67.5 us
  Pallas kernels  65.6 us (97%)
  between operations  1.93 us (3%)
    pallas_call x1, Pallas kernels, per_device(): pl.pallas_call(kernel, out_shape=jax.ShapeDtypeStruct((FIRST, 8, LANES),...  64.6 us

profile of v3, /device:TPU:1, one launch (start us, length us, event | category | flops | bytes accessed | tf_op | source)
XLA Modules:
  0.0 67.5 jit_solution(17860292468920074487)
XLA Ops:
  1.9 64.6 %shard_map.50.acc_ref = f32[32,8,128]{2,1,0:T(8,128)S(1)} custom-call(s32[1]{0:T(128)S(6)} %copy.6.delay_hbm, s32[1]{0:T(128)S(6)} %copy.7.rate_hbm, bf16[8192,128]{1,0:T(8,128)(2,1)} %bitcast.6), custom_call_target="tpu_custom_call" | custom-call | tf_op jit(solution)/shard_map/pallas_call | solution.py:361
  66.5 1.0 %shard_map.51 = (f32[8,32,128]{2,1,0:T(8,128)}, f32[4,128]{1,0:T(4,128)}) custom-call(f32[32,8,128]{2,1,0:T(8,128)S(1)} %shard_map.50.acc_ref), custom_call_target="tpu_custom_call" | custom-call | tf_op jit(solution)/shard_map/pallas_call | solution.py:392

commit v4 on v3

--- a/solution.py
+++ b/solution.py
@@ -274,6 +274,7 @@
             plain = jnp.concatenate([real, imag], axis=2)
             crossed = jnp.concatenate([imag, -real], axis=2)
             both = jnp.concatenate([plain, crossed], axis=1)
+            rows = []
             for quad in range(2):
                 right = plain[4 * quad : 4 * quad + 4].reshape(128, 256)
                 left = both[4 * quad : 4 * quad + 4].reshape(256, 256)
@@ -286,16 +287,17 @@
                 even = jnp.where(low_rows, kept[0], turned[1])
                 odd = jnp.where(low_rows, turned[0], kept[1])
                 mixed = jnp.concatenate([even.reshape(4, 1, 8, LANES), odd.reshape(4, 1, 8, LANES)], axis=1)
-                rs_tx[:, first + i, quad] = mixed.reshape(N_TM, 8, LANES)
+                rows.append(mixed.reshape(N_TM, 8, LANES))
+            rs_tx[:, first + i] = jnp.concatenate(rows, axis=1).astype(jnp.bfloat16)
 
 
     def gather_sums(index):
         at, count = starts[index], CHUNKS[index]
         arrived = rs_rx.at[:, pl.ds(at, count)]
         pltpu.make_async_copy(arrived, arrived, rs_rx_sems.at[index]).wait()
-        total = rs_rx[0, pl.ds(at, count)]
+        total = rs_rx[0, pl.ds(at, count)].astype(jnp.float32)
         for source in range(1, N_TM):
-            total = total + rs_rx[source, pl.ds(at, count)]
+            total = total + rs_rx[source, pl.ds(at, count)].astype(jnp.float32)
         acc_ref[pl.ds(2 * at, 2 * count)] = total.reshape(2 * count, 8, LANES)
 
     for index, (at, count) in enumerate(zip(starts, CHUNKS)):
@@ -375,8 +377,8 @@
             pltpu.VMEM((FIRST, FRAMES_DEV, 256), jnp.bfloat16),
             pltpu.VMEM((STATIONS, PAIRS, 16, LANES), jnp.bfloat16),
             pltpu.VMEM((STATIONS, PAIRS, 16, LANES), jnp.bfloat16),
-            pltpu.VMEM((N_TM, PAIRS, 2, 8, LANES), jnp.float32),
-            pltpu.VMEM((N_TM, PAIRS, 2, 8, LANES), jnp.float32),
+            pltpu.VMEM((N_TM, PAIRS, 16, LANES), jnp.bfloat16),
+            pltpu.VMEM((N_TM, PAIRS, 16, LANES), jnp.bfloat16),
             pltpu.SemaphoreType.DMA((2,)),
             pltpu.SemaphoreType.DMA((8,)),
             pltpu.SemaphoreType.DMA((2,)),

time: 67.6 us -> 67.5 us (level)
  no operation moved by 1% of the time
where the time goes in v4:
time: 67.5 us; the launch traced here: 67.4 us
  Pallas kernels  65.5 us (97%)
  between operations  1.93 us (3%)
    pallas_call x1, Pallas kernels, per_device(): pl.pallas_call(kernel, out_shape=jax.ShapeDtypeStruct((FIRST, 8, LANES),...  64.6 us

profile of v4, /device:TPU:1, one launch (start us, length us, event | category | flops | bytes accessed | tf_op | source)
XLA Modules:
  0.0 67.4 jit_solution(1782741499660748079)
XLA Ops:
  1.9 64.6 %shard_map.50.acc_ref = f32[32,8,128]{2,1,0:T(8,128)S(1)} custom-call(s32[1]{0:T(128)S(6)} %copy.6.delay_hbm, s32[1]{0:T(128)S(6)} %copy.7.rate_hbm, bf16[8192,128]{1,0:T(8,128)(2,1)} %bitcast.6), custom_call_target="tpu_custom_call" | custom-call | tf_op jit(solution)/shard_map/pallas_call | solution.py:363
  66.5 1.0 %shard_map.51 = (f32[8,32,128]{2,1,0:T(8,128)}, f32[4,128]{1,0:T(4,128)}) custom-call(f32[32,8,128]{2,1,0:T(8,128)S(1)} %shard_map.50.acc_ref), custom_call_target="tpu_custom_call" | custom-call | tf_op jit(solution)/shard_map/pallas_call | solution.py:394
